TPU v7x, 512 devices: a whole 4x8x8 slice. The times are simulated.
512 devices in a mesh: seq: 32 (over z, x), dp: 2 (over core), tensor: 8 (over y).
Axes of the slice: x: 4, y: 8, z: 8, core: 2. Of those that a mesh axis runs over, the one named last changes fastest.
Arguments:
- head_inputs: bfloat16 [2, 2560, 16384], P('dp', 'tensor', 'seq'), may hold values from -6 to 6
- b_proj: bfloat16 [2, 16384, 128], P('dp', 'seq'), may hold values from -0.59765625 to 0.59765625
- c_proj: bfloat16 [2, 16384, 128], P('dp', 'seq'), may hold values from -0.59765625 to 0.59765625
- dt_raw: float32 [2, 40, 16384], P('dp', 'tensor', 'seq'), may hold values from -2 to 0
- a_log: float32 [40], P('tensor'), as said below
- d_skip: float32 [40], P('tensor'), may hold values from 0.5 to 1.5
- w_out: bfloat16 [2560, 2560], P('tensor', 'dp'), may hold values from -0.125 to 0.125
- out_grad: bfloat16 [2, 2560, 16384], P('dp', 'tensor', 'seq'), may hold values from -6 to 6
Outputs:
- mixed: bfloat16 [2, 2560, 16384], P('dp', 'tensor', 'seq')
- grad_inputs: bfloat16 [2, 2560, 16384], P('dp', 'tensor', 'seq')
- grad_b: bfloat16 [2, 16384, 128], P('dp', 'seq')
- grad_c: bfloat16 [2, 16384, 128], P('dp', 'seq')
- grad_dt: float32 [2, 40, 16384], P('dp', 'tensor', 'seq')
- grad_alog: float32 [40], P('tensor')
- grad_skip: float32 [40], P('tensor')
- grad_w: bfloat16 [2560, 2560], P('tensor', ('seq', 'dp'))
Inputs may be any that keep to these rules, and one draw needn't show every extreme that they name: exp(a_log) lies between 0.1 / 16384 and 0.1.
All inputs are finite; a program needn't handle non-finite values.
Results may differ from a plain program's by a relative error of at most 0.0049.
Values may be sent and summed in bfloat16 or wider, within the bound.
A program may use at most 128 MiB of HBM per device.

v0:
```python
import jax
import jax.numpy as jnp
from jax import lax
from jax.sharding import PartitionSpec as P

SPAN = 256


HIGH = lax.Precision.HIGHEST


def span_pass(carried, x_block, b_block, c_block, step_block, decay_rate):
    log_decay = step_block * decay_rate[:, None]
    cumulative = jnp.cumsum(log_decay, axis=1)
    block = cumulative.shape[1]
    indices = jnp.arange(block)
    causal = (indices[:, None] >= indices[None, :])[None, :, :]
    spread = cumulative[:, :, None] - cumulative[:, None, :]
    weights = jnp.where(causal, jnp.exp(jnp.where(causal, spread, 0.0)), 0.0)
    affinity = jnp.dot(c_block, b_block.T, precision=HIGH)
    scores = affinity[None, :, :] * weights * step_block[:, None, :]
    block_out = jnp.einsum("hps,hts->hpt", x_block, scores, precision=HIGH)
    block_out = block_out + jnp.exp(cumulative)[:, None, :] * jnp.einsum(
        "hpn,tn->hpt", carried, c_block, precision=HIGH
    )
    tail_weight = jnp.exp(cumulative[:, -1:] - cumulative) * step_block
    updated = jnp.exp(cumulative[:, -1])[:, None, None] * carried
    updated = updated + jnp.einsum(
        "hps,sn->hpn", x_block * tail_weight[:, None, :], b_block, precision=HIGH
    )
    return (updated, block_out)


def sweep(streams, b_rows, c_rows, dt_rows, alog_part, skip_part, state_in):
    head_count, head_width, length = streams.shape
    blocks = length // SPAN
    step_size = jax.nn.softplus(dt_rows)
    decay_rate = -jnp.exp(alog_part)
    x_blocks = streams.reshape(head_count, head_width, blocks, SPAN).transpose(2, 0, 1, 3)
    b_blocks = b_rows.reshape(blocks, SPAN, b_rows.shape[1])
    c_blocks = c_rows.reshape(blocks, SPAN, c_rows.shape[1])
    s_blocks = step_size.reshape(head_count, blocks, SPAN).transpose(1, 0, 2)

    def advance(carried, inputs):
        return span_pass(carried, inputs[0], inputs[1], inputs[2], inputs[3], decay_rate)

    state_end, outputs = lax.scan(advance, state_in, (x_blocks, b_blocks, c_blocks, s_blocks))
    mixed_f = outputs.transpose(1, 2, 0, 3).reshape(head_count, head_width, length)
    return (mixed_f + skip_part[:, None, None] * streams, state_end)


def per_device(head_inputs, b_proj, c_proj, dt_raw, a_log, d_skip, w_out, out_grad):
    head_count = dt_raw.shape[1]
    length = head_inputs.shape[2]
    head_width = head_inputs.shape[1] // head_count
    streams = head_inputs[0].astype(jnp.float32).reshape(head_count, head_width, length)
    b_rows = b_proj[0].astype(jnp.float32)
    c_rows = c_proj[0].astype(jnp.float32)
    dt_rows = dt_raw[0]
    decay_rate = -jnp.exp(a_log)
    step_size = jax.nn.softplus(dt_rows)
    cumulative = jnp.cumsum(step_size * decay_rate[:, None], axis=1)
    device_decay = cumulative[:, -1]
    tail_weight = jnp.exp(device_decay[:, None] - cumulative) * step_size
    local_state = jnp.einsum(
        "hpt,tn->hpn", streams * tail_weight[:, None, :], b_rows, precision=HIGH
    )
    totals = lax.all_gather(device_decay[None, :], "seq", axis=0, tiled=True)
    prefix = jnp.cumsum(totals, axis=0)
    my_index = lax.axis_index("seq")
    reached = lax.dynamic_index_in_dim(prefix, my_index, 0, keepdims=False)
    before = reached - device_decay
    shard_part = lax.all_gather(local_state[None], "seq", axis=0, tiled=True)
    row_count = shard_part.shape[0]
    indices = jnp.arange(row_count, dtype=jnp.int32)
    prefix_ends = prefix
    active = (indices < my_index)[:, None]
    weights = jnp.where(active, jnp.exp(jnp.where(active, before[None, :] - prefix_ends, 0.0)), 0.0)
    state_in = jnp.einsum("jh,jhpn->hpn", weights, shard_part, precision=HIGH)

    def local_sweep(xa, ba, ca, da, aa, sa):
        return sweep(xa, ba, ca, da, aa, sa, state_in)

    primal, pullback = jax.vjp(local_sweep, streams, b_rows, c_rows, dt_rows, a_log, d_skip)
    mixed_half = primal[0].reshape(head_count * head_width, length).astype(jnp.bfloat16)
    g_full = lax.all_gather(out_grad[0], "tensor", axis=0, tiled=True)
    cotan_sum = jnp.dot(
        lax.all_gather(w_out, "dp", axis=1, tiled=True), g_full, preferred_element_type=jnp.float32
    )
    cotan_half = cotan_sum.astype(jnp.bfloat16)
    y_cotan = (
        lax.optimization_barrier(cotan_half)
        .astype(jnp.float32)
        .reshape(head_count, head_width, length)
    )
    local_cotan = jnp.einsum(
        "hpt,tn->hpn", y_cotan * jnp.exp(cumulative)[:, None, :], c_rows, precision=HIGH
    )
    shard_part = lax.all_gather(local_cotan[None], "seq", axis=0, tiled=True)
    row_count = shard_part.shape[0]
    indices = jnp.arange(row_count, dtype=jnp.int32)
    prefix_ends = prefix
    active = (indices > my_index)[:, None]
    weights = jnp.where(
        active, jnp.exp(jnp.where(active, prefix_ends - totals - reached[None, :], 0.0)), 0.0
    )
    cotan_in = jnp.einsum("jh,jhpn->hpn", weights, shard_part, precision=HIGH)
    grads = pullback((y_cotan, cotan_in))
    w_terms = lax.dot_general(
        mixed_half, g_full, (((1,), (1,)), ((), ())), preferred_element_type=jnp.float32
    )
    grad_w = lax.psum_scatter(w_terms, ("seq", "dp"), scatter_dimension=1, tiled=True).astype(
        jnp.bfloat16
    )
    grad_b, grad_c = lax.psum((grads[1], grads[2]), "tensor")
    grad_alog, grad_skip = lax.psum((grads[4], grads[5]), ("seq", "dp"))
    grad_inputs = grads[0].reshape(head_count * head_width, length).astype(jnp.bfloat16)
    return (
        mixed_half[None],
        grad_inputs[None],
        grad_b.astype(jnp.bfloat16)[None],
        grad_c.astype(jnp.bfloat16)[None],
        grads[3][None],
        grad_alog,
        grad_skip,
        grad_w,
    )


def solution(mesh):
    in_specs = (
        P("dp", "tensor", "seq"),
        P("dp", "seq", None),
        P("dp", "seq", None),
        P("dp", "tensor", "seq"),
        P("tensor"),
        P("tensor"),
        P("tensor", "dp"),
        P("dp", "tensor", "seq"),
    )
    out_specs = (
        P("dp", "tensor", "seq"),
        P("dp", "tensor", "seq"),
        P("dp", "seq", None),
        P("dp", "seq", None),
        P("dp", "tensor", "seq"),
        P("tensor"),
        P("tensor"),
        P("tensor", ("seq", "dp")),
    )
    return jax.shard_map(
        per_device, mesh=mesh, in_specs=in_specs, out_specs=out_specs, check_vma=False
    )
```

profile of v0, /device:TPU:24, one launch (start us, length us, event | category | flops | bytes accessed | tf_op | source)
XLA Modules:
  0.0 658.7 jit_solution(519363650831749236)
XLA Ops:
  7.2 0.7 all-gather.9.cloned.1.call-update
  8.0 0.7 all-gather.13.cloned.1.call-update
  9.4 0.8 fusion.149
  10.1 1.5 reduce-window.46
  12.2 0.8 fusion.152
  13.1 1.1 bitcast_multiply_fusion.16
  14.2 1.1 fusion.142
  15.4 17.2 %all-gather.9.cloned.1.call-done = bf16[320,2560]{1,0:T(8,128)(2,1)} async-done(((bf16[320,1280]{1,0:T(8,128)(2,1)}), bf16[320,2560]{1,0:T(8,128)(2,1)}) %all-gather.9.cloned.1.call-update) | async-done | bytes 1638416 | tf_op jit(solution)/shard_map/all_gather | solution.py:88
  32.6 47.6 %all-gather.13.cloned.1.call-done = bf16[1,2560,512]{2,1,0:T(8,128)(2,1)} async-done(((bf16[1,320,512]{2,1,0:T(8,128)(2,1)}), bf16[1,2560,512]{2,1,0:T(8,128)(2,1)}) %all-gather.13.cloned.1.call-update) | async-done | bytes 2621456 | tf_op jit(solution)/shard_map/all_gather | solution.py:86
  80.2 3.2 fusion.131
  83.6 1.1 fusion.140
  85.3 1.3 dynamic-slice
  87.5 76.5 %all-reduce.2 = f32[160]{0:T(256)S(1)} all-reduce(f32[160]{0:T(256)S(1)} %dynamic-update-slice), channel_id=2, replica_groups=mesh['seq'=32,'dp'=2,'tensor'=8] {'seq'}, use_global_device_ids=true, to_apply=%add.2 | all-reduce | flops 160 | bytes 1280
  164.8 1.3 dynamic-slice.1
  167.3 7.4 %all-gather.11.cloned.1.call-done = f32[160,64,128]{2,1,0:T(8,128)} async-done(((f32[5,64,128]{2,1,0:T(8,128)}), f32[160,64,128]{2,1,0:T(8,128)}) %all-gather.11.cloned.1.call-update) | async-done | bytes 5242896 | tf_op jit(solution)/shard_map/all_gather | solution.py:73
  174.6 7.7 %fusion.125 = f32[5,1,64,128]{3,1,2,0:T(1,128)S(1)} fusion(f32[32,5,1,1]{0,2,3,1:T(1,128)S(1)} %copy.117, f32[32,5,64,128]{3,2,1,0:T(8,128)} %bitcast.487), kind=kOutput, calls=%fused_computation.159 | convolution fusion | flops 15728640 | bytes 5407360 | tf_op jit(solution)/shard_map/jh,jhpn->hpn/dot_general | solution.py:79
  182.4 0.9 broadcast.306.clone
  183.3 0.9 broadcast.306.clone.1
  184.2 0.9 broadcast.306.clone.2
  185.1 23.1 %while.75 = (s32[]{:T(128)}, f32[5,64,128]{2,1,0:T(8,128)S(1)}, f32[2,5,64,256]{3,2,1,0:T(8,128)}, f32[2,5,256,256]{3,2,1,0:T(8,128)}, f32[2,128,256]{1,2,0:T(8,...) while((s32[]{:T(128)}, f32[5,64,128]{2,1,0:T(8,128)S(1)}, ...), condition=%wide.region_6.7_spmd.clone.clone, body=%wide.region_3.6_spmd.clone.clone.sunk | while | flops 607838976 | bytes 16159797 | solution.py:47
  185.2 1.5 reduce-window.60
  187.1 1.1 bitcast_dynamic-update-slice_fusion.11
  188.2 2.8 multiply_dynamic-update-slice_fusion.4
  191.2 1.2 bitcast_dynamic-update-slice_fusion.12
  192.4 2.4 fusion.212
  196.0 0.7 bitcast_dynamic-update-slice_fusion.13
  196.8 1.5 reduce-window.60
  198.7 1.1 bitcast_dynamic-update-slice_fusion.11
  199.8 2.8 multiply_dynamic-update-slice_fusion.4
  202.8 1.2 bitcast_dynamic-update-slice_fusion.12
  204.0 2.4 fusion.212
  208.2 1.6 copy.110
  209.8 1.4 reshape.722
  211.3 5.4 fusion.127
  216.7 0.9 add_convert_fusion.1
  217.6 47.9 %all-gather.15.cloned.1.call-done = f32[160,64,128]{2,1,0:T(8,128)} async-done(((f32[5,64,128]{2,1,0:T(8,128)}), f32[160,64,128]{2,1,0:T(8,128)}) %all-gather.15.cloned.1.call-update) | async-done | bytes 5242896 | tf_op jit(solution)/shard_map/all_gather | solution.py:99
  265.5 7.7 %fusion.123 = f32[5,1,64,128]{3,1,2,0:T(1,128)S(1)} fusion(f32[32,5,1,1]{0,2,3,1:T(1,128)S(1)} %copy.120, f32[32,5,64,128]{3,2,1,0:T(8,128)} %bitcast.486), kind=kOutput, calls=%fused_computation.157 | convolution fusion | flops 15728640 | bytes 5407360 | tf_op jit(solution)/shard_map/jh,jhpn->hpn/dot_general | solution.py:107
  273.2 0.9 broadcast.306
  274.1 0.7 broadcast.313
  274.9 0.7 broadcast.313.clone
  275.6 46.3 %while.76 = (s32[]{:T(128)}, f32[5]{0:T(128)S(1)}, f32[5,64,128]{2,1,0:T(8,128)S(1)}, f32[2,5,64,256]{3,2,1,0:T(8,128)}, f32[2,256,128]{2,1,0:T(8,128)}, /*index...) while((s32[]{:T(128)}, f32[5]{0:T(128)S(1)}, ...), condition=%wide.region_19.20_spmd.clone.clone, body=%wide.region_7.19_spmd.clone.clone.sunk | while | flops 1212566272 | bytes 13529267 | solution.py:47
  275.6 1.0 dynamic-slice_bitcast_fusion.8
  276.6 3.9 fusion.227
  281.5 1.0 fusion.228
  282.6 6.3 reduce-window.62
  289.3 0.8 convolution_bitcast_fusion.6
  290.1 1.9 fusion.240
  292.3 1.8 convolution_bitcast_fusion.5
  294.1 1.2 fusion.239
  295.3 3.0 fusion.238
  298.8 1.0 dynamic-slice_bitcast_fusion.8
  299.8 3.9 fusion.227
  304.7 1.0 fusion.228
  305.8 6.3 reduce-window.62
  312.5 0.8 convolution_bitcast_fusion.6
  313.3 1.9 fusion.240
  315.5 1.8 convolution_bitcast_fusion.5
  317.2 1.3 fusion.239
  318.5 3.0 fusion.238
  322.0 1.6 copy.114
  323.7 0.9 fusion.134
  324.7 0.7 exponential_multiply_fusion.1
  325.5 290.5 %all-reduce.8 = (f32[5]{0:T(128)}, f32[5]{0:T(128)}, bf16[320,2560]{0,1:T(8,128)(2,1)S(1)}) all-reduce(f32[5]{0:T(128)S(1)} %negate_multiply_fusion, f32[5]{0:T(128)S(1)} %reduce_sum.212, f32[320,2560]{0,1:T(8,128)} %fusion.127), channel_id=1, replica_groups=mesh['seq'=32,'dp'=2,'tensor'=8] {'seq','dp'}, use_global_device_ids=true, to_apply=%region_22.23 | all-reduce | flops 819210 | bytes 4915280 | tf_op jit(solution)/shard_map/psum | solution.py:116
  616.7 35.5 %all-reduce.9 = (bf16[512,128]{1,0:T(8,128)(2,1)}, bf16[512,128]{1,0:T(8,128)(2,1)}) all-reduce(f32[512,128]{1,0:T(8,128)S(1)} %bitcast.502, f32[512,128]{1,0:T(8,128)S(1)} %bitcast.503), channel_id=1, replica_groups=mesh['seq'=32,'dp'=2,'tensor'=8] {'tensor'}, use_global_device_ids=true, to_apply=%region_20.21 | all-reduce | flops 131072 | bytes 786432 | tf_op jit(solution)/shard_map/psum | solution.py:115
  (192 shorter events, 13.2 us)
Async XLA Ops:
  7.2 7.0 %copy-start.8 = (bf16[1,512,128]{2,1,0:T(8,128)(2,1)S(1)}, bf16[1,512,128]{2,1,0:T(8,128)(2,1)}, u32[]{:S(2)}) copy-start(bf16[1,512,128]{2,1,0:T(8,128)(2,1)} %param.13) | copy-start | bytes 393220
  7.2 25.4 %all-gather.9.cloned.1.call-start = ((), (), s32[]{:S(2)}) async-start(), calls=%async_computation | async-start | bytes 2457600 | tf_op jit(solution)/shard_map/all_gather | solution.py:88
  7.9 72.3 %all-gather.13.cloned.1.call-start = ((), (), s32[]{:S(2)}) async-start(), calls=%async_computation.2 | async-start | bytes 2949120 | tf_op jit(solution)/shard_map/all_gather | solution.py:86
  8.7 166.0 %all-gather.11.cloned.1.call-start = ((), (), s32[]{:S(2)}) async-start(), calls=%async_computation.1 | async-start | bytes 5406720 | tf_op jit(solution)/shard_map/all_gather | solution.py:73
  15.3 68.2 %copy-start.9 = (bf16[1,512,128]{2,1,0:T(8,128)(2,1)S(1)}, bf16[1,512,128]{2,1,0:T(8,128)(2,1)}, u32[]{:S(2)}) copy-start(bf16[1,512,128]{2,1,0:T(8,128)(2,1)} %param.14) | copy-start | bytes 393220
  15.3 69.4 %copy-start = (bf16[1,320,512]{2,1,0:T(8,128)(2,1)S(1)}, bf16[1,320,512]{2,1,0:T(8,128)(2,1)}, u32[]{:S(2)}) copy-start(bf16[1,320,512]{2,1,0:T(8,128)(2,1)} %param.12) | copy-start | bytes 983044
  15.3 250.1 %all-gather.15.cloned.1.call-start = ((), (), s32[]{:S(2)}) async-start(), calls=%async_computation.3 | async-start | bytes 5406720 | tf_op jit(solution)/shard_map/all_gather | solution.py:99
  83.5 83.3 %copy-start.3 = (bf16[320,512]{1,0:T(8,128)(2,1)}, bf16[320,512]{1,0:T(8,128)(2,1)S(1)}, u32[]{:S(2)}) copy-start(bf16[320,512]{1,0:T(8,128)(2,1)S(1)} %fusion.131) | copy-start | bytes 983044
  83.5 81.0 %copy-start.10 = (f32[1,5,512]{2,0,1:T(1,128)S(1)}, f32[1,5,512]{2,0,1:T(1,128)}, u32[]{:S(2)}) copy-start(f32[1,5,512]{2,0,1:T(1,128)} %param.15) | copy-start | bytes 30724
  83.5 81.2 %copy-start.11 = (f32[5]{0:T(128)S(1)}, f32[5]{0:T(128)}, u32[]{:S(2)}) copy-start(f32[5]{0:T(128)} %param.17) | copy-start | bytes 64
  191.2 3.7 copy-start.1
  194.9 0.8 copy-start.2
  202.8 3.6 copy-start.1
  206.4 0.8 copy-start.2
  211.2 5.4 copy-start.5
  321.9 1.7 copy-start.4
  321.9 2.7 copy-start.12
  323.7 293.0 %copy-start.6 = (f32[2,256,128]{2,1,0:T(8,128)S(1)}, f32[2,256,128]{2,1,0:T(8,128)}, u32[]{:S(2)}) copy-start(f32[2,256,128]{2,1,0:T(8,128)} %get-tuple-element.972) | copy-start | bytes 786436
  323.7 293.0 %copy-start.7 = (f32[2,256,128]{2,1,0:T(8,128)S(1)}, f32[2,256,128]{2,1,0:T(8,128)}, u32[]{:S(2)}) copy-start(f32[2,256,128]{2,1,0:T(8,128)} %get-tuple-element.973) | copy-start | bytes 786436
Sparse Core Ops, SparseCore 0:
  10.1 22.4 all-gather.8
  34.6 45.5 all-gather.12
  83.9 90.6 all-gather.10
  177.7 87.7 all-gather.14
where the time goes:
time: 660 us; the launch traced here: 659 us
  blocking collectives  403 us (61%)
  waiting for transfers between devices  121 us (18%)
  matrix products  63.7 us (10%)
  other arithmetic  33.6 us (5%)
  local copies, waits for them, and re-layouts  21.4 us (3%)
  between operations  15.6 us (2%)
    psum x1, blocking collectives, per_device(): grad_alog, grad_skip = lax.psum((grads[4], grads[5]), ('seq', 'dp'))  291 us
    unnamed x1, blocking collectives  76.5 us
    all_gather x1, waiting for transfers between devices, per_device(): shard_part = lax.all_gather(local_cotan[None], 'seq', axis=0, tiled=True)  47.9 us
    all_gather x1, waiting for transfers between devices, per_device(): g_full = lax.all_gather(out_grad[0], 'tensor', axis=0, tiled=True)  47.6 us
    psum x1, blocking collectives, per_device(): grad_b, grad_c = lax.psum((grads[1], grads[2]), 'tensor')  35.5 us
    dot_general x6, matrix products, span_pass(): block_out = jnp.einsum('hps,hts->hpt', x_block, scores, precision=HIGH)  18.5 us
    another operation x23, other arithmetic  17.6 us
    all_gather x1, waiting for transfers between devices, per_device(): lax.all_gather(w_out, 'dp', axis=1, tiled=True)  17.2 us
  transfers between devices with their start and end apart: 4, of which 4 were waited for; matrix products, arithmetic and copies ran while one was open for 9% of the time, Pallas kernels for 0%

commit v1 on v0

v1 whole, which is shorter than its diff:
```python
import functools
import types

import jax
import jax.numpy as jnp
from jax import lax
from jax.experimental import pallas as pl
from jax.experimental.pallas import tpu as pltpu
from jax.sharding import PartitionSpec as P

F32 = jnp.float32
BF16 = jnp.bfloat16
CHUNKS = 4
NN = (((1,), (0,)), ((), ()))
NT = (((1,), (1,)), ((), ()))
TN = (((0,), (0,)), ((), ()))


def mul(a, b, dims):
    return lax.dot_general(a, b, dims, preferred_element_type=F32)


def split(v):
    hi = v.astype(BF16)
    return hi, (v - hi.astype(F32)).astype(BF16)


def mul3(a, b, dims):
    return mul(a[0], b[0], dims) + mul(a[1], b[0], dims) + mul(a[0], b[1], dims)


def mul2(a, b, dims):
    return mul(a[0], b, dims) + mul(a[1], b, dims)


def prefix_sum(v, reverse=False):
    length = v.shape[1]
    lane = lax.broadcasted_iota(jnp.int32, v.shape, 1)
    shift = 1
    while shift < length:
        if reverse:
            moved = pltpu.roll(v, length - shift, 1)
            v = v + jnp.where(lane < length - shift, moved, 0.0)
        else:
            moved = pltpu.roll(v, shift, 1)
            v = v + jnp.where(lane >= shift, moved, 0.0)
        shift *= 2
    return v


def space(d):
    return types.SimpleNamespace(**{k: space(v) if isinstance(v, dict) else v for k, v in d.items()})


def kernel(dims, names, tree, *refs):
    nz, nx, ny, heads, width, length, state = dims
    r = space(
        dict(zip(names, refs[: len(names)], strict=True))
        | jax.tree.unflatten(tree, refs[len(names) :])
    )
    x_ref, b_ref, c_ref = r.x_in, r.b_in, r.c_in
    rows_all = heads * width
    rp = width // nx
    fx = rows_all // nx
    seq = lax.axis_index("seq")
    core = lax.axis_index("dp")
    y = lax.axis_index("tensor")
    z = lax.div(seq, nx)
    x = lax.rem(seq, nx)
    sends, stores = [], []

    def wrap(i, n):
        return lax.rem(i + n, n)

    def copy(src, dst, ch, out, into, where):
        return pltpu.make_async_remote_copy(
            src_ref=src,
            dst_ref=dst,
            send_sem=ch.s.at[out],
            recv_sem=ch.r.at[into],
            device_id=where,
            device_id_type=pl.DeviceIdType.MESH,
        )

    def start(*a):
        c = copy(*a)
        c.start()
        sends.append(c)

    def at_x(i):
        return {"seq": z * nx + i}

    def at_z(i):
        return {"seq": i * nx + x}

    def at_y(i):
        return {"tensor": i}

    other = {"dp": 1 - core}

    def exchange(n, me, place, src, dst, ch):
        for k in range(1, n):
            p = wrap(me + k, n)
            start(src(p), dst(me), ch, (p,), (me,), place(p))

    def arrived(n, me, place, src, dst, ch):
        for k in range(1, n):
            p = wrap(me + k, n)
            copy(src(p), dst(p), ch, (p,), (p,), place(p)).wait_recv()

    def store(src, dst):
        c = pltpu.make_async_copy(src, dst, r.stores.at[len(stores)])
        c.start()
        stores.append(c)

    def head(h):
        return slice(h * width, (h + 1) * width)

    g_all = r.g_all
    own_rows = g_all.at[pl.ds(pl.multiple_of(y * rows_all, 16), rows_all), :]
    loads = [
        pltpu.make_async_copy(src, dst, r.load.at[i])
        for i, (src, dst) in enumerate(
            ((r.dt, r.dt_in), (r.x, x_ref), (r.b, b_ref), (r.c, c_ref), (r.w, r.w_in), (r.g, own_rows))
        )
    ]
    for c in loads:
        c.start()

    barrier = pltpu.get_barrier_semaphore()
    peers = [at_x(wrap(x + k, nx)) for k in range(1, nx)]
    peers += [at_z(wrap(z + k, nz)) for k in range(1, nz)]
    peers += [at_y(wrap(y + k, ny)) for k in range(1, ny)] + [other]
    for p in peers:
        pl.semaphore_signal(barrier, inc=1, device_id=p, device_id_type=pl.DeviceIdType.MESH)
    pl.semaphore_wait(barrier, len(peers))

    far = ny // 2
    tall = rows_all // CHUNKS

    def block(t, c):
        return g_all.at[pl.ds(pl.multiple_of(t * rows_all + c * tall, 16), tall), :]

    def forward(k, c, way):
        if k + 1 > far or (k + 1 == far and (c < CHUNKS // 2) != (way == 0)):
            return
        t = wrap(y - k, ny) if way == 0 else wrap(y + k, ny)
        to = wrap(y + 1, ny) if way == 0 else wrap(y - 1, ny)
        src = r.g.at[pl.ds(c * tall, tall), :] if k == 0 else block(t, c)
        start(src, block(t, c), r.ch.g, (way, k, c,), (t, c,), at_y(to))

    def block_in(t, c):
        copy(block(t, c), block(t, c), r.ch.g, (0, 0, 0,), (t, c,), at_y(y)).wait_recv()

    def relay(k, chunks):
        for c in chunks:
            if k == far:
                block_in(wrap(y + k, ny), c)
                continue
            block_in(wrap(y - k, ny), c)
            forward(k, c, 0)
            block_in(wrap(y + k, ny), c)
            forward(k, c, 1)

    for c in range(CHUNKS):
        forward(0, c, 0)
        forward(0, c, 1)
    start(r.w, r.w_other, r.ch.w, (0,), (0,), other)

    tile = r.dt_rows
    tile[...] = jnp.zeros_like(tile)
    loads[0].wait()
    for h in range(heads):
        tile[h : h + 1, :] = r.dt_in[h]
    rate_rows = r.rate_rows
    rate_rows[...] = jnp.zeros_like(rate_rows)
    for h in range(heads):
        rate_rows[h : h + 1, :] = -jnp.exp(jnp.full((1, length), r.alog[h], F32))
    dt = tile[...]
    rate = rate_rows[...]
    grown = jnp.exp(dt)
    step = jnp.log(1.0 + grown)
    log_decay = step * rate
    cum = prefix_sum(log_decay)
    up = jnp.exp(cum)
    into = step * jnp.exp(-cum)
    decay_x, decay_z = r.decay_x, r.decay_z
    decay_x[x] = jnp.broadcast_to(up[:, length - 1 : length], (8, 128))
    exchange(nx, x, at_x, lambda p: decay_x.at[x], lambda p: decay_x.at[p], r.ch.dx)

    xs_h, xs_l = r.xs_h, r.xs_l
    loads[1].wait()
    for h in range(heads):
        hi, lo = split(x_ref[head(h), :].astype(F32) * into[h : h + 1, :])
        xs_h[head(h), :] = hi
        xs_l[head(h), :] = lo

    loads[2].wait()
    part = mul2((xs_h[...], xs_l[...]), b_ref[...], NN)
    mine = decay_x[x]
    ends = r.ends
    for h in range(heads):
        ends[h] = part[head(h), :] * mine[h : h + 1, :]

    def piece(ref, i):
        return ref.at[:, pl.ds(pl.multiple_of(i * rp, rp), rp), :]

    def cut(ref, i):
        return ref[:, pl.ds(pl.multiple_of(i * rp, rp), rp), :]

    def along_x(src, st):
        got = st.got1
        exchange(nx, x, at_x, lambda p: piece(src, p), lambda p: got.at[p], st.ch1)
        got[x] = cut(src, x)

    def along_z(src, st, back):
        got, tot = st.got1, st.tot
        arrived(nx, x, at_x, lambda p: piece(src, p), lambda p: got.at[p], st.ch1)
        for h in range(heads):
            acc = jnp.zeros((rp, state), F32)
            for j in reversed(range(nx)) if back else range(nx):
                acc = acc * decay_x[j, h : h + 1, :] + got[j, h].astype(F32)
            tot[h] = acc.astype(tot.dtype)
        for k in range(1, nz):
            p = z - k if back else z + k

            @pl.when(p >= 0 if back else p < nz)
            def _(p=p):
                copy(tot, st.got2.at[z], st.ch2, (p,), (z,), at_z(p)).start()

    def back_along_x(dst, st, back):
        got, tot, acc, out = st.got1, st.tot, st.acc, st.got3
        acc[...] = jnp.zeros_like(acc)

        def gather(i, carry):
            p = nz - 1 - i if back else i
            slot = st.got2.at[p]
            copy(tot, slot, st.ch2, (p,), (p,), at_z(p)).wait_recv()
            for h in range(heads):
                acc[h] = acc[h] * decay_z[p, h : h + 1, :] + st.got2[p, h].astype(F32)
            return carry

        lax.fori_loop(0, nz - 1 - z if back else z, gather, 0)
        for h in range(heads):
            s = acc[h]
            for j in reversed(range(nx)) if back else range(nx):
                out[j, h] = s.astype(out.dtype)
                s = s * decay_x[j, h : h + 1, :] + got[j, h].astype(F32)
        for k in range(1, nx):
            p = wrap(x + k, nx)
            start(out.at[p], piece(dst, x), st.ch3, (p,), (x,), at_x(p))
        dst[:, pl.ds(pl.multiple_of(x * rp, rp), rp), :] = out[x]

    def in_from_x(dst, st):
        for k in range(1, nx):
            p = wrap(x + k, nx)
            copy(st.got3.at[p], piece(dst, p), st.ch3, (p,), (p,), at_x(p)).wait_recv()

    def z_sent(st, back):
        for k in range(1, nz):
            p = z - k if back else z + k

            @pl.when(p >= 0 if back else p < nz)
            def _(p=p):
                copy(st.tot, st.got2.at[z], st.ch2, (p,), (z,), at_z(p)).wait_send()

    along_x(ends, r.ahead)
    arrived(nx, x, at_x, lambda p: decay_x.at[x], lambda p: decay_x.at[p], r.ch.dx)
    group = decay_x[0]
    for j in range(1, nx):
        group = group * decay_x[j]
    decay_z[z] = group
    exchange(nz, z, at_z, lambda p: decay_z.at[z], lambda p: decay_z.at[p], r.ch.dz)

    loads[3].wait()
    earlier = lax.broadcasted_iota(jnp.int32, (length, length), 0) >= lax.broadcasted_iota(
        jnp.int32, (length, length), 1
    )
    near_h, near_l = r.near_h, r.near_l
    hi, lo = split(jnp.where(earlier, mul(c_ref[...], b_ref[...], NT), 0.0))
    near_h[...] = hi
    near_l[...] = lo

    w_block, cotan_f = r.w_block, r.cotan_f
    per_core = ny // 2

    def w_blocks(ref, d):
        for i in range(per_core):
            w_block[d * per_core + i] = ref[:, i * rows_all : (i + 1) * rows_all]

    def term(k):
        t = wrap(y + k, ny)
        return mul(w_block[t], g_all[pl.ds(pl.multiple_of(t * rows_all, 16), rows_all), :], NN)

    early, late = range(CHUNKS // 2), range(CHUNKS // 2, CHUNKS)
    if far > 1:
        relay(1, early)
    along_z(ends, r.ahead, False)
    if far > 1:
        relay(1, late)
    loads[4].wait()
    w_blocks(r.w_in, core)
    copy(r.w, r.w_other, r.ch.w, (0,), (0,), other).wait_recv()
    w_blocks(r.w_other, 1 - core)
    loads[5].wait()
    cotan_f[...] = term(0)
    if far > 1:
        cotan_f[...] += term(1) + term(-1)
    arrived(nz, z, at_z, lambda p: decay_z.at[z], lambda p: decay_z.at[p], r.ch.dz)
    start_state = r.start_state
    if far > 2:
        relay(2, range(CHUNKS))
        cotan_f[...] += term(2) + term(-2)
    back_along_x(start_state, r.ahead, False)
    if far > 3:
        relay(3, range(CHUNKS))
        cotan_f[...] += term(3) + term(-3)
    in_from_x(start_state, r.ahead)

    s_h, s_l = split(start_state[...].reshape(rows_all, state))
    r.s_h[...] = s_h
    r.s_l[...] = s_l
    summed = mul3((xs_h[...], xs_l[...]), (near_h[...], near_l[...]), NT) + mul2((s_h, s_l), c_ref[...], NT)
    mixed = r.mixed
    past = r.past
    for h in range(heads):
        v = summed[head(h), :] * up[h : h + 1, :]
        past[head(h), :] = v
        mixed[head(h), :] = (v + r.skip[h] * x_ref[head(h), :].astype(F32)).astype(BF16)

    store(mixed, r.to_mixed)

    evens = [0] + [s * k for k in range(2, far, 2) for s in (1, -1)] + ([far] if far % 2 == 0 else [])
    odds = [s * k for k in range(1, far, 2) for s in (1, -1)] + ([far] if far % 2 == 1 else [])
    same = lax.rem(y + core, 2) == 0
    gw_dp, gw_out, gw_send, gw_x, gw_z = r.gw_dp, r.gw_out, r.gw_send, r.gw_x, r.gw_z

    def product(t):
        return mul(g_all[pl.ds(pl.multiple_of(t * rows_all, 16), rows_all), :], mixed[...], NT)

    def kept(j):
        return wrap(jnp.where(same, y + evens[j], y + odds[j]), ny)

    def w_pair(j):
        t = wrap(jnp.where(same, y + odds[j], y + evens[j]), ny)
        gw_out[j] = product(t).astype(BF16)
        start(gw_out.at[j], gw_dp.at[j], r.ch.wd, (j,), (j,), other)
        r.gw_own[j] = product(kept(j))

    def w_rows(j, p):
        return gw_send.at[j, pl.ds(pl.multiple_of(p * fx, 16), fx), :]

    def w_along_x(j):
        copy(gw_out.at[j], gw_dp.at[j], r.ch.wd, (j,), (j,), other).wait_recv()
        gw_send[j] = (r.gw_own[j] + gw_dp[j].astype(F32)).astype(BF16)
        for k in range(1, nx):
            p = wrap(x + k, nx)
            start(w_rows(j, p), gw_x.at[j, x], r.ch.wx, (j, p,), (j, x,), at_x(p))

    def w_along_z(j):
        total = gw_send[j, pl.ds(pl.multiple_of(x * fx, 16), fx), :].astype(F32)
        for k in range(1, nx):
            p = wrap(x + k, nx)
            copy(w_rows(j, p), gw_x.at[j, p], r.ch.wx, (j, p,), (j, p,), at_x(p)).wait_recv()
            total = total + gw_x[j, p].astype(F32)
        t = kept(j)
        gw_z_out = r.gw_z_out
        gw_z_out[j] = total.astype(BF16)

        @pl.when(t == z)
        def _():
            gw_z[z] = gw_z_out[j]

        @pl.when(t != z)
        def _():
            copy(gw_z_out.at[j], gw_z.at[z], r.ch.wz, (j,), (z,), at_z(t)).start()

    pairs = len(evens)
    for j in range(pairs - 1):
        w_pair(j)
    relay(far, range(CHUNKS))

    cotan = r.cotan
    cotan[...] = (cotan_f[...] + term(far)).astype(BF16)
    cs_h, cs_l = r.cs_h, r.cs_l
    for h in range(heads):
        hi, lo = split(cotan[head(h), :].astype(F32) * up[h : h + 1, :])
        cs_h[head(h), :] = hi
        cs_l[head(h), :] = lo
    starts = r.starts
    starts[...] = mul2((cs_h[...], cs_l[...]), c_ref[...], NN).reshape(heads, width, state).astype(starts.dtype)
    along_x(starts, r.behind)

    for j in range(pairs - 1):
        w_along_x(j)
    w_pair(pairs - 1)

    hi, lo = split(jnp.where(earlier, mul3((cs_h[...], cs_l[...]), (xs_h[...], xs_l[...]), TN), 0.0))
    near_gh, near_gl = r.near_gh, r.near_gl
    near_gh[...] = hi
    near_gl[...] = lo
    along_z(starts, r.behind, True)

    piece_rows = length // ny

    def tokens(ref, p):
        return ref.at[pl.ds(pl.multiple_of(p * piece_rows, 16), piece_rows), :]

    grad_c = mul2((near_gh[...], near_gl[...]), b_ref[...], NN) + mul3(
        (cs_h[...], cs_l[...]), (r.s_h[...], r.s_l[...]), TN
    )

    def over_y(v, st):
        send = st.out
        send[...] = v.astype(BF16)
        exchange(ny, y, at_y, lambda p: tokens(send, p), lambda p: st.got.at[p], st.ch)

    def back_over_y(st):
        send, got, full = st.out, st.got, st.full
        arrived(ny, y, at_y, lambda p: tokens(send, p), lambda p: got.at[p], st.ch)
        total = send[pl.ds(pl.multiple_of(y * piece_rows, 16), piece_rows), :].astype(F32)
        for k in range(1, ny):
            total = total + got[wrap(y + k, ny)].astype(F32)
        full[pl.ds(pl.multiple_of(y * piece_rows, 16), piece_rows), :] = total.astype(BF16)
        exchange(ny, y, at_y, lambda p: tokens(full, y), lambda p: tokens(full, p), st.chf)

    def in_over_y(st, out):
        full = st.full
        arrived(ny, y, at_y, lambda p: tokens(full, y), lambda p: tokens(full, p), st.chf)
        store(full, out)

    over_y(grad_c, r.sgc)
    w_along_x(pairs - 1)

    xg = r.xg
    xg[...] = mul3((cs_h[...], cs_l[...]), (near_h[...], near_l[...]), NN)
    grad_b = r.grad_b
    grad_b[...] = mul2((near_gh[...], near_gl[...]), c_ref[...], TN)
    to_in, to_cum, end_part, head_part = r.to_in, r.to_cum, r.end_part, r.head_part
    for ref in (to_in, to_cum, end_part, head_part):
        ref[...] = jnp.zeros_like(ref)
    total = cum[:, length - 1 : length]
    left_h, left_l = r.left_h, r.left_l
    for h in range(heads):
        xf = x_ref[head(h), :].astype(F32)
        gf = cotan[head(h), :].astype(F32)
        xs = xf * into[h : h + 1, :]
        inner = jnp.sum(xg[head(h), :] * xs, axis=0, keepdims=True)
        here = jnp.sum(gf * r.past[head(h), :], axis=0, keepdims=True) - inner
        to_cum[h : h + 1, :] = here
        skip_sum = jnp.sum(jnp.sum(gf * xf, axis=0, keepdims=True), axis=1, keepdims=True)
        decay_sum = jnp.sum(here * cum[h : h + 1, :], axis=1, keepdims=True)
        spot = lax.broadcasted_iota(jnp.int32, (1, 128), 1) == h
        head_part[0:1, :] += jnp.where(spot, decay_sum, 0.0)
        head_part[1:2, :] += jnp.where(spot, skip_sum, 0.0)
        hi, lo = split(xs * (total[h : h + 1, :] - cum[h : h + 1, :]))
        left_h[head(h), :] = hi
        left_l[head(h), :] = lo
    weigh = r.weigh
    weigh[...] = mul2((left_h[...], left_l[...]), b_ref[...], NN)
    for h in range(heads):
        weigh[head(h), :] = (weigh[head(h), :] + total[h : h + 1, :] * start_state[h]) * mine[h : h + 1, :]

    end_cotan = r.end_cotan
    back_along_x(end_cotan, r.behind, True)
    back_over_y(r.sgc)
    for j in range(pairs):
        w_along_z(j)
    in_from_x(end_cotan, r.behind)

    scaled = r.scaled
    for h in range(heads):
        scaled[head(h), :] = end_cotan[h].astype(F32) * mine[h : h + 1, :]
    e = split(scaled[...])
    over_y(grad_b[...] + mul3((xs_h[...], xs_l[...]), e, TN), r.sgb)
    hx, hz, hd = r.hx, r.hz, r.hd
    for h in range(heads):
        by_lane = jnp.sum(end_cotan[h].astype(F32) * weigh[head(h), :], axis=0, keepdims=True)
        spot = lax.broadcasted_iota(jnp.int32, (1, 128), 1) == h
        head_part[0:1, :] += jnp.where(spot, jnp.sum(by_lane, axis=1, keepdims=True), 0.0)
    hx[x] = head_part[...]
    exchange(nx, x, at_x, lambda p: hx.at[x], lambda p: hx.at[p], r.ch.hx)

    later = mul2(e, b_ref[...], NT)
    for h in range(heads):
        xf = x_ref[head(h), :].astype(F32)
        gf = cotan[head(h), :].astype(F32)
        d_later = later[head(h), :] * into[h : h + 1, :]
        d = xg[head(h), :] * into[h : h + 1, :] + d_later
        r.gx[head(h), :] = (d + r.skip[h] * gf).astype(BF16)
        to_in[h : h + 1, :] = jnp.sum(d * xf, axis=0, keepdims=True)
        to_cum[h : h + 1, :] -= jnp.sum(d_later * xf, axis=0, keepdims=True)
        closing = start_state[h] * mine[h : h + 1, :] + ends[h]
        end_part[h : h + 1, :] = jnp.sum(end_cotan[h].astype(F32) * closing, axis=0, keepdims=True)
    decay_grad = prefix_sum(to_cum[...], reverse=True) + jnp.sum(end_part[...], axis=1, keepdims=True)
    step_grad = rate * decay_grad + to_in[...] / step
    step_grad = step_grad * (grown / (1.0 + grown))
    for h in range(heads):
        r.gdt[h] = step_grad[h : h + 1, :]
    store(r.gx, r.to_gx)
    store(r.gdt, r.to_gdt)

    arrived(nx, x, at_x, lambda p: hx.at[x], lambda p: hx.at[p], r.ch.hx)
    both = hx[0]
    for j in range(1, nx):
        both = both + hx[j]
    hz[z] = both
    exchange(nz, z, at_z, lambda p: hz.at[z], lambda p: hz.at[p], r.ch.hz)
    back_over_y(r.sgb)
    in_over_y(r.sgc, r.to_gc)
    arrived(nz, z, at_z, lambda p: hz.at[z], lambda p: hz.at[p], r.ch.hz)
    both = hz[0]
    for j in range(1, nz):
        both = both + hz[j]
    hd[0] = both
    start(hd.at[0], hd.at[1], r.ch.hd, (0,), (0,), other)

    own_half = fx // 2
    gw_sum, gw_fin = r.gw_sum, r.gw_fin

    def final(d):
        return gw_sum.at[pl.ds(pl.multiple_of(d * own_half, 8), own_half), :]

    def final_copy():
        return copy(final(1 - core), gw_fin, r.ch.wf, (0,), (0,), other)

    owner = lax.rem(z + core, 2) == 0

    @pl.when(owner)
    def _():
        for k in range(1, nz):
            p = wrap(z + k, nz)
            copy(r.gw_z_out.at[0], gw_z.at[p], r.ch.wz, (0,), (p,), at_z(p)).wait_recv()
        total = gw_z[0].astype(F32)
        for j in range(1, nz):
            total = total + gw_z[j].astype(F32)
        gw_sum[...] = total
        final_copy().start()
        r.gwt[...] = gw_sum[pl.ds(pl.multiple_of(core * own_half, 8), own_half), :].astype(BF16)
        final_copy().wait_send()

    @pl.when(jnp.logical_not(owner))
    def _():
        final_copy().wait_recv()
        r.gwt[...] = gw_fin[...].astype(BF16)

    store(r.gwt, r.to_gwt)
    in_over_y(r.sgb, r.to_gb)
    copy(hd.at[0], hd.at[1], r.ch.hd, (0,), (0,), other).wait_recv()
    r.small[...] = hd[0] + hd[1]
    store(r.small, r.to_small)

    for c in stores:
        c.wait()
    for c in sends:
        c.wait_send()
    z_sent(r.ahead, False)
    z_sent(r.behind, True)
    for j in range(pairs):
        t = kept(j)

        @pl.when(t != z)
        def _(j=j, t=t):
            copy(r.gw_z_out.at[j], gw_z.at[z], r.ch.wz, (j,), (z,), at_z(t)).wait_send()


def build(nz, nx, ny, heads, width, length, state):
    rows = heads * width
    fx = rows // nx
    rp = width // nx
    pairs = ny // 2
    far = ny // 2
    piece = length // ny
    vm = pltpu.VMEM
    dma = pltpu.SemaphoreType.DMA

    def channel(sent, received=None):
        return dict(s=dma(sent), r=dma(received or sent))

    def chain(kind):
        return dict(
            got1=vm((nx, heads, rp, state), kind),
            got2=vm((nz, heads, rp, state), kind),
            got3=vm((nx, heads, rp, state), kind),
            tot=vm((heads, rp, state), kind),
            acc=vm((heads, rp, state), F32),
            ch1=channel((nx,)),
            ch2=channel((nz,)),
            ch3=channel((nx,)),
        )

    def summed():
        return dict(
            out=vm((length, state), BF16),
            got=vm((ny, piece, state), BF16),
            full=vm((length, state), BF16),
            ch=channel((ny,)),
            chf=channel((ny,)),
        )

    scratch = dict(
        g_all=vm((ny * rows, length), BF16),
        w_other=vm((rows, ny * rows // 2), BF16),
        dt_rows=vm((8, length), F32),
        rate_rows=vm((8, length), F32),
        to_in=vm((8, length), F32),
        to_cum=vm((8, length), F32),
        head_part=vm((8, 128), F32),
        dt_in=vm((heads, 1, length), F32),
        x_in=vm((rows, length), BF16),
        b_in=vm((length, state), BF16),
        c_in=vm((length, state), BF16),
        w_in=vm((rows, ny * rows // 2), BF16),
        w_block=vm((ny, rows, rows), BF16),
        cotan_f=vm((rows, length), F32),
        left_h=vm((rows, length), BF16),
        left_l=vm((rows, length), BF16),
        weigh=vm((rows, state), F32),
        grad_b=vm((length, state), F32),
        load=dma((6,)),
        end_part=vm((8, state), F32),
        decay_x=vm((nx, 8, 128), F32),
        decay_z=vm((nz, 8, 128), F32),
        hx=vm((nx, 8, 128), F32),
        hz=vm((nz, 8, 128), F32),
        hd=vm((2, 8, 128), F32),
        xs_h=vm((rows, length), BF16),
        xs_l=vm((rows, length), BF16),
        cs_h=vm((rows, length), BF16),
        cs_l=vm((rows, length), BF16),
        cotan=vm((rows, length), BF16),
        past=vm((rows, length), F32),
        xg=vm((rows, length), F32),
        near_h=vm((length, length), BF16),
        near_l=vm((length, length), BF16),
        near_gh=vm((length, length), BF16),
        near_gl=vm((length, length), BF16),
        ends=vm((heads, width, state), F32),
        start_state=vm((heads, width, state), F32),
        starts=vm((heads, width, state), BF16),
        end_cotan=vm((heads, width, state), BF16),
        s_h=vm((rows, state), BF16),
        s_l=vm((rows, state), BF16),
        scaled=vm((rows, state), F32),
        gw_out=vm((pairs, rows, rows), BF16),
        gw_dp=vm((pairs, rows, rows), BF16),
        gw_own=vm((pairs, rows, rows), F32),
        gw_send=vm((pairs, rows, rows), BF16),
        gw_x=vm((pairs, nx, fx, rows), BF16),
        gw_z=vm((nz, fx, rows), BF16),
        gw_z_out=vm((pairs, fx, rows), BF16),
        gw_sum=vm((fx, rows), F32),
        gw_fin=vm((fx // 2, rows), F32),
        ahead=chain(F32),
        behind=chain(BF16),
        sgc=summed(),
        sgb=summed(),
        ch=dict(
            g=channel((2, far, CHUNKS), (ny, CHUNKS)),
            w=channel((1,)),
            dx=channel((nx,)),
            dz=channel((nz,)),
            wd=channel((pairs,)),
            wx=channel((pairs, nx)),
            wz=channel((pairs,), (nz,)),
            wf=channel((1,)),
            hx=channel((nx,)),
            hz=channel((nz,)),
            hd=channel((1,)),
        ),
    )
    vmem = pl.BlockSpec(memory_space=pltpu.VMEM)
    smem = pl.BlockSpec(memory_space=pltpu.SMEM)
    hbm = pl.BlockSpec(memory_space=pl.ANY)
    ins = dict(x=hbm, b=hbm, c=hbm, dt=hbm, alog=smem, skip=smem, w=hbm, g=hbm)
    outs = dict(
        mixed=((rows, length), BF16),
        gx=((rows, length), BF16),
        gb=((length, state), BF16),
        gc=((length, state), BF16),
        gdt=((heads, 1, length), F32),
        gwt=((fx // 2, rows), BF16),
        small=((8, 128), F32),
    )
    scratch |= {k: vm(*v) for k, v in outs.items() if k not in ("gb", "gc")}
    scratch["stores"] = dma((len(outs),))
    placed_at = ["to_" + k for k in outs]
    held, inner = jax.tree.flatten(scratch, is_leaf=lambda v: not isinstance(v, dict))
    return pl.pallas_call(
        functools.partial(
            kernel, (nz, nx, ny, heads, width, length, state), list(ins) + placed_at, inner
        ),
        out_shape=[jax.ShapeDtypeStruct(s, d) for s, d in outs.values()],
        in_specs=list(ins.values()),
        out_specs=[hbm] * len(outs),
        scratch_shapes=held,
        compiler_params=pltpu.CompilerParams(
            collective_id=0, has_side_effects=True, vmem_limit_bytes=56 * 2**20
        ),
    )


def write_out(small, *refs):
    decay, skip, sems = refs[-3:]
    half = len(refs) // 2 - 1
    copies = [
        pltpu.make_async_copy(src, dst, sems.at[i])
        for i, (src, dst) in enumerate(zip(refs[:half], refs[half:-3], strict=True))
    ]
    for c in copies:
        c.start()
    decay[...] = small[0:1, 0 : decay.shape[1]]
    skip[...] = small[1:2, 0 : skip.shape[1]]
    for c in copies:
        c.wait()


def placed(results, small, heads):
    row = jax.ShapeDtypeStruct((1, heads), F32)
    vmem, hbm = pl.BlockSpec(memory_space=pltpu.VMEM), pl.BlockSpec(memory_space=pl.ANY)
    return pl.pallas_call(
        write_out,
        out_shape=[jax.ShapeDtypeStruct(v.shape, v.dtype) for v in results] + [row, row],
        in_specs=[vmem] * (len(results) + 1),
        out_specs=[hbm] * len(results) + [vmem, vmem],
        scratch_shapes=[pltpu.SemaphoreType.DMA((len(results),))],
    )(small, *results)


def solution(mesh):
    ny = mesh.shape["tensor"]
    nz = ny
    nx = mesh.shape["seq"] // nz

    def per_device(head_inputs, b_proj, c_proj, dt_raw, a_log, d_skip, w_out, out_grad):
        heads, length = dt_raw.shape[1:]
        width = head_inputs.shape[1] // heads
        call = build(nz, nx, ny, heads, width, length, b_proj.shape[2])
        *results, small = call(
            head_inputs[0],
            b_proj[0],
            c_proj[0],
            dt_raw.transpose(1, 0, 2),
            a_log,
            d_skip,
            w_out,
            out_grad[0],
        )
        mixed, gx, gb, gc, gdt, gwt, decay, skip = placed(results, small, heads)
        return (
            mixed[None],
            gx[None],
            gb[None],
            gc[None],
            gdt.transpose(1, 0, 2),
            decay[0],
            skip[0],
            gwt.T,
        )

    rows, tokens, per_head = P("dp", "tensor", "seq"), P("dp", "seq", None), P("tensor")
    return jax.shard_map(
        per_device,
        mesh=mesh,
        in_specs=(rows, tokens, tokens, rows, per_head, per_head, P("tensor", "dp"), rows),
        out_specs=(rows, rows, tokens, tokens, rows, per_head, per_head, P("tensor", ("seq", "dp"))),
        check_vma=False,
    )
```

time: 660 us -> 76.4 us (0.12)
  the two profiles are of different devices: /device:TPU:24 before, /device:TPU:84 now
where the time goes in v1:
time: 76.4 us; the launch traced here: 76.2 us
  Pallas kernels  75.6 us (99%)
    pallas_call x1, Pallas kernels, per_device(): call(head_inputs[0], b_proj[0], c_proj[0], dt_raw.transpose(1, 0, 2), a_l...  72.9 us
    pallas_call x1, Pallas kernels, placed(): pl.pallas_call(write_out, out_shape=[jax.ShapeDtypeStruct(v.shape, v.dtyp...  2.68 us

profile of v1, /device:TPU:84, one launch (start us, length us, event | category | flops | bytes accessed | tf_op | source)
XLA Modules:
  0.0 76.2 jit_solution(11721861857464673258)
XLA Ops:
  0.6 72.9 %shard_map.143 = (bf16[320,512]{1,0:T(8,128)(2,1)}, bf16[320,512]{1,0:T(8,128)(2,1)}, bf16[512,128]{1,0:T(8,128)(2,1)}, bf16[512,128]{1,0:T(8,128)(2,1)}, f32[5,...) custom-call(bf16[320,512]{1,0:T(8,128)(2,1)} %bitcast.13, bf16[512,128]{1,0:T(8,128)(2,1)} %bitcast.15, ...), custom_call_target="tpu_custom_call" | custom-call | tf_op jit(solution)/shard_map/pallas_call | solution.py:739
  73.5 2.7 %shard_map.144 = (bf16[320,512]{1,0:T(8,128)(2,1)}, bf16[320,512]{1,0:T(8,128)(2,1)}, bf16[512,128]{1,0:T(8,128)(2,1)}, bf16[512,128]{1,0:T(8,128)(2,1)}, f32[5,...) custom-call(f32[8,128]{1,0:T(8,128)} %get-tuple-element.23.small, ...), custom_call_target="tpu_custom_call" | custom-call | tf_op jit(solution)/shard_map/pallas_call | solution.py:721

commit v2 on v1

--- a/solution.py
+++ b/solution.py
@@ -108,6 +108,11 @@
             p = wrap(me + k, n)
             copy(src(p), dst(p), ch, (p,), (p,), place(p)).wait_recv()
 
+    def left(n):
+        for c in sends[:n]:
+            c.wait_send()
+        del sends[:n]
+
     def store(src, dst):
         c = pltpu.make_async_copy(src, dst, r.stores.at[len(stores)])
         c.start()
@@ -127,13 +132,30 @@
     for c in loads:
         c.start()
 
+    def beside(n):
+        return (1,) if n == 2 else (1, n - 1) if n > 1 else ()
+
     barrier = pltpu.get_barrier_semaphore()
-    peers = [at_x(wrap(x + k, nx)) for k in range(1, nx)]
-    peers += [at_z(wrap(z + k, nz)) for k in range(1, nz)]
-    peers += [at_y(wrap(y + k, ny)) for k in range(1, ny)] + [other]
+    axes = ((at_y, y, ny), (at_x, x, nx), (at_z, z, nz))
+    peers = [other] + [place(wrap(i + k, n)) for place, i, n in axes for k in beside(n)]
     for p in peers:
         pl.semaphore_signal(barrier, inc=1, device_id=p, device_id_type=pl.DeviceIdType.MESH)
     pl.semaphore_wait(barrier, len(peers))
+
+    def tell(word, stage, place, i, n):
+        if stage < n // 2 - 1:
+            for way, k in enumerate((1, n - 1)):
+                pl.semaphore_signal(
+                    word.at[stage, way],
+                    inc=1,
+                    device_id=place(wrap(i + k, n)),
+                    device_id_type=pl.DeviceIdType.MESH,
+                )
+
+    def told(word, stage, n):
+        if stage < n // 2 - 1:
+            for way in range(2):
+                pl.semaphore_wait(word.at[stage, way], 1)
 
     far = ny // 2
     tall = rows_all // CHUNKS
@@ -166,6 +188,8 @@
         forward(0, c, 0)
         forward(0, c, 1)
     start(r.w, r.w_other, r.ch.w, (0,), (0,), other)
+    tell(r.word_x, 0, at_x, x, nx)
+    tell(r.word_z, 0, at_z, z, nz)
 
     tile = r.dt_rows
     tile[...] = jnp.zeros_like(tile)
@@ -186,7 +210,12 @@
     into = step * jnp.exp(-cum)
     decay_x, decay_z = r.decay_x, r.decay_z
     decay_x[x] = jnp.broadcast_to(up[:, length - 1 : length], (8, 128))
+    for stage in range(nx // 2 - 1):
+        told(r.word_x, stage, nx)
+        tell(r.word_x, stage + 1, at_x, x, nx)
     exchange(nx, x, at_x, lambda p: decay_x.at[x], lambda p: decay_x.at[p], r.ch.dx)
+    told(r.word_z, 0, nz)
+    tell(r.word_z, 1, at_z, z, nz)
 
     xs_h, xs_l = r.xs_h, r.xs_l
     loads[1].wait()
@@ -194,6 +223,9 @@
         hi, lo = split(x_ref[head(h), :].astype(F32) * into[h : h + 1, :])
         xs_h[head(h), :] = hi
         xs_l[head(h), :] = lo
+
+    told(r.word_z, 1, nz)
+    tell(r.word_z, 2, at_z, z, nz)
 
     loads[2].wait()
     part = mul2((xs_h[...], xs_l[...]), b_ref[...], NN)
@@ -270,6 +302,9 @@
     for j in range(1, nx):
         group = group * decay_x[j]
     decay_z[z] = group
+    for stage in range(2, nz // 2 - 1):
+        told(r.word_z, stage, nz)
+        tell(r.word_z, stage + 1, at_z, z, nz)
     exchange(nz, z, at_z, lambda p: decay_z.at[z], lambda p: decay_z.at[p], r.ch.dz)
 
     loads[3].wait()
@@ -317,6 +352,10 @@
         cotan_f[...] += term(3) + term(-3)
     in_from_x(start_state, r.ahead)
 
+    xt_h, xt_l = r.xt_h, r.xt_l
+    xt_h[...] = xs_h[...].T
+    xt_l[...] = xs_l[...].T
+
     s_h, s_l = split(start_state[...].reshape(rows_all, state))
     r.s_h[...] = s_h
     r.s_l[...] = s_l
@@ -378,6 +417,7 @@
     pairs = len(evens)
     for j in range(pairs - 1):
         w_pair(j)
+    before_far = len(sends)
     relay(far, range(CHUNKS))
 
     cotan = r.cotan
@@ -461,18 +501,23 @@
     for h in range(heads):
         weigh[head(h), :] = (weigh[head(h), :] + total[h : h + 1, :] * start_state[h]) * mine[h : h + 1, :]
 
+    left(before_far)
+    z_sent(r.ahead, False)
+    before_end = len(sends)
     end_cotan = r.end_cotan
     back_along_x(end_cotan, r.behind, True)
     back_over_y(r.sgc)
     for j in range(pairs):
         w_along_z(j)
+    left(before_end)
+    before_last = len(sends)
     in_from_x(end_cotan, r.behind)
 
     scaled = r.scaled
     for h in range(heads):
         scaled[head(h), :] = end_cotan[h].astype(F32) * mine[h : h + 1, :]
     e = split(scaled[...])
-    over_y(grad_b[...] + mul3((xs_h[...], xs_l[...]), e, TN), r.sgb)
+    over_y(grad_b[...] + mul3((xt_h[...], xt_l[...]), e, NN), r.sgb)
     hx, hz, hd = r.hx, r.hz, r.hd
     for h in range(heads):
         by_lane = jnp.sum(end_cotan[h].astype(F32) * weigh[head(h), :], axis=0, keepdims=True)
@@ -492,14 +537,10 @@
         to_cum[h : h + 1, :] -= jnp.sum(d_later * xf, axis=0, keepdims=True)
         closing = start_state[h] * mine[h : h + 1, :] + ends[h]
         end_part[h : h + 1, :] = jnp.sum(end_cotan[h].astype(F32) * closing, axis=0, keepdims=True)
-    decay_grad = prefix_sum(to_cum[...], reverse=True) + jnp.sum(end_part[...], axis=1, keepdims=True)
-    step_grad = rate * decay_grad + to_in[...] / step
-    step_grad = step_grad * (grown / (1.0 + grown))
-    for h in range(heads):
-        r.gdt[h] = step_grad[h : h + 1, :]
     store(r.gx, r.to_gx)
-    store(r.gdt, r.to_gdt)
-
+
+    left(before_last)
+    z_sent(r.behind, True)
     arrived(nx, x, at_x, lambda p: hx.at[x], lambda p: hx.at[p], r.ch.hx)
     both = hx[0]
     for j in range(1, nx):
@@ -507,6 +548,37 @@
     hz[z] = both
     exchange(nz, z, at_z, lambda p: hz.at[z], lambda p: hz.at[p], r.ch.hz)
     back_over_y(r.sgb)
+
+    decay_grad = prefix_sum(to_cum[...], reverse=True) + jnp.sum(end_part[...], axis=1, keepdims=True)
+    step_grad = rate * decay_grad + to_in[...] / step
+    step_grad = step_grad * (grown / (1.0 + grown))
+    for h in range(heads):
+        r.gdt[h] = step_grad[h : h + 1, :]
+    store(r.gdt, r.to_gdt)
+
+    own_half = fx // 2
+    gw_sum, gw_fin = r.gw_sum, r.gw_fin
+
+    def final(d):
+        return gw_sum.at[pl.ds(pl.multiple_of(d * own_half, 8), own_half), :]
+
+    def final_copy():
+        return copy(final(1 - core), gw_fin, r.ch.wf, (0,), (0,), other)
+
+    owner = lax.rem(z + core, 2) == 0
+
+    @pl.when(owner)
+    def _():
+        total = jnp.zeros((fx, rows_all), F32)
+        for k in range(1, nz):
+            p = wrap(z + k, nz)
+            copy(r.gw_z_out.at[0], gw_z.at[p], r.ch.wz, (0,), (p,), at_z(p)).wait_recv()
+        for j in range(nz):
+            total = total + gw_z[j].astype(F32)
+        gw_sum[...] = total
+        final_copy().start()
+        r.gwt[...] = gw_sum[pl.ds(pl.multiple_of(core * own_half, 8), own_half), :].astype(BF16)
+
     in_over_y(r.sgc, r.to_gc)
     arrived(nz, z, at_z, lambda p: hz.at[z], lambda p: hz.at[p], r.ch.hz)
     both = hz[0]
@@ -515,28 +587,8 @@
     hd[0] = both
     start(hd.at[0], hd.at[1], r.ch.hd, (0,), (0,), other)
 
-    own_half = fx // 2
-    gw_sum, gw_fin = r.gw_sum, r.gw_fin
-
-    def final(d):
-        return gw_sum.at[pl.ds(pl.multiple_of(d * own_half, 8), own_half), :]
-
-    def final_copy():
-        return copy(final(1 - core), gw_fin, r.ch.wf, (0,), (0,), other)
-
-    owner = lax.rem(z + core, 2) == 0
-
     @pl.when(owner)
     def _():
-        for k in range(1, nz):
-            p = wrap(z + k, nz)
-            copy(r.gw_z_out.at[0], gw_z.at[p], r.ch.wz, (0,), (p,), at_z(p)).wait_recv()
-        total = gw_z[0].astype(F32)
-        for j in range(1, nz):
-            total = total + gw_z[j].astype(F32)
-        gw_sum[...] = total
-        final_copy().start()
-        r.gwt[...] = gw_sum[pl.ds(pl.multiple_of(core * own_half, 8), own_half), :].astype(BF16)
         final_copy().wait_send()
 
     @pl.when(jnp.logical_not(owner))
@@ -545,6 +597,13 @@
         r.gwt[...] = gw_fin[...].astype(BF16)
 
     store(r.gwt, r.to_gwt)
+    for j in range(pairs):
+        t = kept(j)
+
+        @pl.when(t != z)
+        def _(j=j, t=t):
+            copy(r.gw_z_out.at[j], gw_z.at[z], r.ch.wz, (j,), (z,), at_z(t)).wait_send()
+
     in_over_y(r.sgb, r.to_gb)
     copy(hd.at[0], hd.at[1], r.ch.hd, (0,), (0,), other).wait_recv()
     r.small[...] = hd[0] + hd[1]
@@ -552,16 +611,7 @@
 
     for c in stores:
         c.wait()
-    for c in sends:
-        c.wait_send()
-    z_sent(r.ahead, False)
-    z_sent(r.behind, True)
-    for j in range(pairs):
-        t = kept(j)
-
-        @pl.when(t != z)
-        def _(j=j, t=t):
-            copy(r.gw_z_out.at[j], gw_z.at[z], r.ch.wz, (j,), (z,), at_z(t)).wait_send()
+    left(len(sends))
 
 
 def build(nz, nx, ny, heads, width, length, state):
@@ -618,6 +668,8 @@
         weigh=vm((rows, state), F32),
         grad_b=vm((length, state), F32),
         load=dma((6,)),
+        word_x=pltpu.SemaphoreType.REGULAR((max(nx // 2 - 1, 1), 2)),
+        word_z=pltpu.SemaphoreType.REGULAR((max(nz // 2 - 1, 1), 2)),
         end_part=vm((8, state), F32),
         decay_x=vm((nx, 8, 128), F32),
         decay_z=vm((nz, 8, 128), F32),
@@ -627,6 +679,8 @@
         xs_h=vm((rows, length), BF16),
         xs_l=vm((rows, length), BF16),
         cs_h=vm((rows, length), BF16),
+        xt_h=vm((length, rows), BF16),
+        xt_l=vm((length, rows), BF16),
         cs_l=vm((rows, length), BF16),
         cotan=vm((rows, length), BF16),
         past=vm((rows, length), F32),

time: 76.4 us -> 75.2 us (0.984)
  the two profiles are of different devices: /device:TPU:84 before, /device:TPU:16 now
where the time goes in v2:
time: 75.2 us; the launch traced here: 75 us
  Pallas kernels  74.4 us (99%)
    pallas_call x1, Pallas kernels, per_device(): call(head_inputs[0], b_proj[0], c_proj[0], dt_raw.transpose(1, 0, 2), a_l...  71.7 us
    pallas_call x1, Pallas kernels, placed(): pl.pallas_call(write_out, out_shape=[jax.ShapeDtypeStruct(v.shape, v.dtyp...  2.68 us

profile of v2, /device:TPU:16, one launch (start us, length us, event | category | flops | bytes accessed | tf_op | source)
XLA Modules:
  0.0 75.0 jit_solution(3782012734688823596)
XLA Ops:
  0.6 71.7 %shard_map.143 = (bf16[320,512]{1,0:T(8,128)(2,1)}, bf16[320,512]{1,0:T(8,128)(2,1)}, bf16[512,128]{1,0:T(8,128)(2,1)}, bf16[512,128]{1,0:T(8,128)(2,1)}, f32[5,...) custom-call(bf16[320,512]{1,0:T(8,128)(2,1)} %bitcast.13, bf16[512,128]{1,0:T(8,128)(2,1)} %bitcast.15, ...), custom_call_target="tpu_custom_call" | custom-call | tf_op jit(solution)/shard_map/pallas_call | solution.py:793
  72.3 2.7 %shard_map.144 = (bf16[320,512]{1,0:T(8,128)(2,1)}, bf16[320,512]{1,0:T(8,128)(2,1)}, bf16[512,128]{1,0:T(8,128)(2,1)}, bf16[512,128]{1,0:T(8,128)(2,1)}, f32[5,...) custom-call(f32[8,128]{1,0:T(8,128)} %get-tuple-element.23.small, ...), custom_call_target="tpu_custom_call" | custom-call | tf_op jit(solution)/shard_map/pallas_call | solution.py:775

commit v3 on v2

--- a/solution.py
+++ b/solution.py
@@ -99,7 +99,7 @@
     other = {"dp": 1 - core}
 
     def exchange(n, me, place, src, dst, ch):
-        for k in range(1, n):
+        for k in sorted(range(1, n), key=lambda k: -min(k, n - k)):
             p = wrap(me + k, n)
             start(src(p), dst(me), ch, (p,), (me,), place(p))
 
@@ -253,7 +253,7 @@
             for j in reversed(range(nx)) if back else range(nx):
                 acc = acc * decay_x[j, h : h + 1, :] + got[j, h].astype(F32)
             tot[h] = acc.astype(tot.dtype)
-        for k in range(1, nz):
+        for k in sorted(range(1, nz), key=lambda k: -min(k, nz - k)):
             p = z - k if back else z + k
 
             @pl.when(p >= 0 if back else p < nz)
@@ -278,7 +278,7 @@
             for j in reversed(range(nx)) if back else range(nx):
                 out[j, h] = s.astype(out.dtype)
                 s = s * decay_x[j, h : h + 1, :] + got[j, h].astype(F32)
-        for k in range(1, nx):
+        for k in sorted(range(1, nx), key=lambda k: -min(k, nx - k)):
             p = wrap(x + k, nx)
             start(out.at[p], piece(dst, x), st.ch3, (p,), (x,), at_x(p))
         dst[:, pl.ds(pl.multiple_of(x * rp, rp), rp), :] = out[x]
@@ -431,8 +431,6 @@
     starts[...] = mul2((cs_h[...], cs_l[...]), c_ref[...], NN).reshape(heads, width, state).astype(starts.dtype)
     along_x(starts, r.behind)
 
-    for j in range(pairs - 1):
-        w_along_x(j)
     w_pair(pairs - 1)
 
     hi, lo = split(jnp.where(earlier, mul3((cs_h[...], cs_l[...]), (xs_h[...], xs_l[...]), TN), 0.0))
@@ -440,6 +438,9 @@
     near_gh[...] = hi
     near_gl[...] = lo
     along_z(starts, r.behind, True)
+    soon = min(3, pairs)
+    for j in range(soon):
+        w_along_x(j)
 
     piece_rows = length // ny
 
@@ -470,7 +471,6 @@
         store(full, out)
 
     over_y(grad_c, r.sgc)
-    w_along_x(pairs - 1)
 
     xg = r.xg
     xg[...] = mul3((cs_h[...], cs_l[...]), (near_h[...], near_l[...]), NN)
@@ -506,8 +506,10 @@
     before_end = len(sends)
     end_cotan = r.end_cotan
     back_along_x(end_cotan, r.behind, True)
+    for j in range(soon, pairs):
+        w_along_x(j)
     back_over_y(r.sgc)
-    for j in range(pairs):
+    for j in range(soon):
         w_along_z(j)
     left(before_end)
     before_last = len(sends)
@@ -538,6 +540,8 @@
         closing = start_state[h] * mine[h : h + 1, :] + ends[h]
         end_part[h : h + 1, :] = jnp.sum(end_cotan[h].astype(F32) * closing, axis=0, keepdims=True)
     store(r.gx, r.to_gx)
+    for j in range(soon, pairs):
+        w_along_z(j)
 
     left(before_last)
     z_sent(r.behind, True)

time: 75.2 us -> 73.6 us (0.979)
  the two profiles are of different devices: /device:TPU:16 before, /device:TPU:24 now
where the time goes in v3:
time: 73.6 us; the launch traced here: 72.3 us
  Pallas kernels  71.7 us (97%)
    pallas_call x1, Pallas kernels, per_device(): call(head_inputs[0], b_proj[0], c_proj[0], dt_raw.transpose(1, 0, 2), a_l...  69 us
    pallas_call x1, Pallas kernels, placed(): pl.pallas_call(write_out, out_shape=[jax.ShapeDtypeStruct(v.shape, v.dtyp...  2.68 us

profile of v3, /device:TPU:24, one launch (start us, length us, event | category | flops | bytes accessed | tf_op | source)
XLA Modules:
  0.0 72.3 jit_solution(18440217402848704718)
XLA Ops:
  0.6 69.0 %shard_map.143 = (bf16[320,512]{1,0:T(8,128)(2,1)}, bf16[320,512]{1,0:T(8,128)(2,1)}, bf16[512,128]{1,0:T(8,128)(2,1)}, bf16[512,128]{1,0:T(8,128)(2,1)}, f32[5,...) custom-call(bf16[320,512]{1,0:T(8,128)(2,1)} %bitcast.13, bf16[512,128]{1,0:T(8,128)(2,1)} %bitcast.15, ...), custom_call_target="tpu_custom_call" | custom-call | tf_op jit(solution)/shard_map/pallas_call | solution.py:797
  69.6 2.7 %shard_map.144 = (bf16[320,512]{1,0:T(8,128)(2,1)}, bf16[320,512]{1,0:T(8,128)(2,1)}, bf16[512,128]{1,0:T(8,128)(2,1)}, bf16[512,128]{1,0:T(8,128)(2,1)}, f32[5,...) custom-call(f32[8,128]{1,0:T(8,128)} %get-tuple-element.23.small, ...), custom_call_target="tpu_custom_call" | custom-call | tf_op jit(solution)/shard_map/pallas_call | solution.py:779
